TPU v7x, 256 devices: a whole 4x4x8 slice. The times are simulated.
256 devices in a mesh: row: 64 (over z, y, core), col: 4 (over x).
Axes of the slice: x: 4, y: 4, z: 8, core: 2. Of those that a mesh axis runs over, the one named last changes fastest.
Arguments:
- panel_col: float32 [131072, 256], P('row', 'col'), may hold values from -6 to 6
- look_cols: float32 [131072, 2048], P('row', 'col'), may hold values from -6 to 6
- sketch_map: float32 [256, 131072], P(None, 'row'), may hold values from -0.015625 to 0.015625
- upper_inv: float32 [256, 256], replicated, may hold values from -0.09375 to 0.09375
- lower_inv: float32 [256, 256], replicated, may hold values from -0.375 to 0.375
- pivots: int32 [256], replicated, may hold values from 256 to 131071, as said below
Outputs:
- l_panel: float32 [131072, 256], P('row', 'col')
- updated: float32 [131072, 2048], P('row', 'col')
- sketch: float32 [256, 256], P(None, 'col')
Inputs may be any that keep to these rules, and one draw needn't show every extreme that they name: `pivots`: distinct rows, none of them among the first 256.
All inputs are finite; a program needn't handle non-finite values.
Results may differ from a plain program's by a relative error of at most 0.000073.
Values sent between devices are 32-bit elements; how exact they have to be, the bound alone decides.
A program may use at most 64 MiB of HBM per device.

v0:
```python
import jax
import jax.numpy as jnp
from jax import lax
from jax.sharding import PartitionSpec as P

high_prec = lax.Precision.HIGHEST


def on_device(panel_col, look_cols, sketch_map, upper_inv, lower_inv, pivots):
    row_count = panel_col.shape[0]
    col_width = panel_col.shape[1]
    block_size = upper_inv.shape[0]
    col_index = lax.axis_index("col")
    row_index = lax.axis_index("row")
    first_row = row_index * row_count
    owned = (pivots >= first_row) & (pivots < first_row + row_count)
    local_idx = jnp.where(owned, pivots - first_row, 0)
    owned_mask = owned[:, None]
    panel_pick = jnp.where(owned_mask, panel_col[local_idx], 0.0)
    look_pick = jnp.where(owned_mask, look_cols[local_idx], 0.0)
    sketch_part = jnp.dot(
        sketch_map, panel_col, precision=high_prec, preferred_element_type=jnp.float32
    )
    on_root = row_index == 0
    panel_head = jnp.where(on_root, panel_col[:block_size], 0.0)
    look_head = jnp.where(on_root, look_cols[:block_size], 0.0)
    sketch, panel_piv, look_piv, panel_orig, look_orig = lax.psum(
        (sketch_part, panel_pick, look_pick, panel_head, look_head), "row"
    )
    target = jnp.where(owned, pivots - first_row, row_count)
    swapped_panel = panel_col.at[target].set(panel_orig, mode="drop")
    swapped_look = look_cols.at[target].set(look_orig, mode="drop")
    swapped_panel = jnp.where(on_root, swapped_panel.at[:block_size].set(panel_piv), swapped_panel)
    swapped_look = jnp.where(on_root, swapped_look.at[:block_size].set(look_piv), swapped_look)
    upper_tri = jnp.triu(upper_inv)
    lower_tri = jnp.tril(lower_inv, -1) + jnp.eye(block_size, dtype=jnp.float32)
    upper_rows = lax.dynamic_slice_in_dim(upper_tri, col_index * col_width, col_width, 0)
    partial_prod = jnp.dot(
        swapped_panel, upper_rows, precision=high_prec, preferred_element_type=jnp.float32
    )
    factor = lax.psum(partial_prod, "col")
    global_row = first_row + jnp.arange(row_count, dtype=jnp.int32)
    is_top = (global_row < block_size)[:, None]
    my_factor = lax.dynamic_slice_in_dim(factor, col_index * col_width, col_width, 1)
    l_panel = jnp.where(is_top, swapped_panel, my_factor)
    u_rows = jnp.dot(lower_tri, look_piv, precision=high_prec, preferred_element_type=jnp.float32)
    updated = swapped_look - jnp.dot(
        factor, u_rows, precision=high_prec, preferred_element_type=jnp.float32
    )
    updated = jnp.where(on_root, updated.at[:block_size].set(u_rows), updated)
    return (l_panel, updated, sketch)


def solution(mesh):
    placed = (P("row", "col"), P("row", "col"), P(None, "row"), P(), P(), P())
    return jax.shard_map(
        on_device,
        mesh=mesh,
        in_specs=placed,
        out_specs=(P("row", "col"), P("row", "col"), P(None, "col")),
        check_vma=False,
    )
```

profile of v0, /device:TPU:1, one launch (start us, length us, event | category | flops | bytes accessed | tf_op | source)
XLA Modules:
  0.0 307.5 jit_solution(13693479291795300407)
XLA Ops:
  7.2 0.0 copy-start
  7.2 0.0 copy-start.5
  7.2 0.0 all-reduce.6.cloned.1.call-start
  7.2 4.8 %copy.27 = f32[2048,512]{1,0:T(8,128)} copy(f32[2048,512]{1,0:T(8,128)} %param.13) | data formatting | bytes 8388608
  12.0 0.0 copy-done.5
  12.1 1.4 copy.10
  13.4 0.0 copy-done
  13.5 3.7 %fusion.14 = f32[256,64]{0,1:T(8,128)} fusion(f32[256,2048]{1,0:T(8,128)S(1)} %copy-done, f32[2048,64]{0,1:T(8,128)} %param.12), kind=kOutput, calls=%fused_computation.36 | convolution fusion | flops 402653184 | bytes 2686976 | tf_op jit(solution)/shard_map/dot_general | solution.py:21
  17.2 0.7 gather_fusion
  17.9 4.2 %gather_fusion.1 = f32[256,512]{1,0:T(8,128)} fusion(f32[2048,512]{1,0:T(8,128)} %copy.27, s32[1024]{0:T(1024)S(1)} %pad_clamp_fusion), kind=kCustom, calls=%fused_computation.1 | custom fusion | bytes 1049600 | tf_op jit(solution)/shard_map/gather | solution.py:20
  22.1 0.7 slice_select_fusion.4
  22.8 2.3 slice_select_fusion.2
  25.1 0.0 all-reduce.6.cloned.1.call-update
  25.1 0.0 all-reduce.4.cloned.1.call-start
  25.2 0.1 iota_compare_fusion.1
  25.3 190.4 %all-reduce.6.cloned.1.call-done = (f32[256,64]{1,0:T(8,128)}, f32[256,64]{1,0:T(8,128)}, f32[256,512]{1,0:T(8,128)}, f32[256,512]{1,0:T(8,128)}, f32[256,64]{0,1:T(8,128)}) async-done(((f32[256,64]{1,0:T(8,128)}, f32[256,64]{1,0:T(8,128)}, f32[256,512]{1,0:T(8,128)}, f32[256,512]{1,0:T(8,128)}, f32[256,64]{0,1:T(8,128)}), (f32[256,64]{1,0:T(8,128)}, f32[256,64]{1,0:T(8,128)}, f32[256,512]{1,0:T(8,128)}, ...) | async-done | bytes 1245200 | tf_op jit(solution)/shard_map/psum | solution.py:27
  215.7 1.9 scatter_fusion
  217.7 3.9 %fusion.8 = f32[2048,256]{1,0:T(8,128)} fusion(f32[2048,64]{1,0:T(8,128)S(1)} %fusion.6, f32[256,256]{1,0:T(8,128)} %param.15, s32[]{:T(128)S(6)} %select_n.87, pred[256,256]{1,0:T(32,128)(4,1)S(1)} %iota_compare_fusion.1), kind=kOutput, calls=%fused_computation.23 | convolution fusion | flops 402669568 | bytes 3227652 | tf_op jit(solution)/shard_map/dot_general | solution.py:38
  221.6 0.0 all-reduce.4.cloned.1.call-update
  221.7 0.0 copy-start.3
  221.7 6.1 %scatter_fusion.1 = f32[2048,512]{1,0:T(8,128)} fusion(f32[2048,512]{1,0:T(8,128)} %copy.27, s32[256]{0:T(256)S(1)} %get-tuple-element.48, f32[256,512]{1,0:T(8,128)} %get-tuple-element.44), kind=kCustom, calls=%fused_computation.3 | custom fusion | bytes 1573888 | tf_op jit(solution)/shard_map/scatter | solution.py:32
  227.8 0.0 copy-done.3
  227.8 2.5 fusion.2
  230.3 1.9 fusion.1
  232.2 53.3 %all-reduce.4.cloned.1.call-done = f32[2048,256]{1,0:T(8,128)} async-done(((f32[2048,256]{1,0:T(8,128)}), f32[2048,256]{1,0:T(8,128)}) %all-reduce.4.cloned.1.call-update) | async-done | bytes 2097168 | tf_op jit(solution)/shard_map/psum | solution.py:41
  285.5 8.7 %convolution_subtract_fusion = f32[2048,512]{1,0:T(8,128)} fusion(f32[2048,512]{1,0:T(8,128)} %fusion.1, f32[2048,256]{1,0:T(8,128)} %all-reduce.4.cloned.1.call-done, f32[256,512]{1,0:T(8,128)} %fusion.2), kind=kOutput, calls=%fused_computation.4 | convolution fusion | flops 3222274048 | bytes 11010048 | tf_op jit(solution)/shard_map/dot_general | solution.py:47
  294.1 0.0 copy-done.2
  294.1 1.9 fusion
  296.1 0.0 copy-done.1
  296.1 1.6 dynamic-slice_select_fusion
  297.7 2.3 copy.12
  300.0 0.6 copy.28
  (10 shorter events, 0.1 us)
Async XLA Ops:
  7.2 6.3 %copy-start = (f32[256,2048]{1,0:T(8,128)S(1)}, f32[256,2048]{1,0:T(8,128)}, u32[]{:S(2)}) copy-start(f32[256,2048]{1,0:T(8,128)} %param.14) | copy-start | bytes 6291460
  7.2 4.8 %copy-start.5 = (s32[256]{0:T(256)S(1)}, s32[256]{0:T(256)}, u32[]{:S(2)}) copy-start(s32[256]{0:T(256)} %param.17) | copy-start | bytes 3076
  7.2 208.5 %all-reduce.6.cloned.1.call-start = ((), (), s32[]{:S(2)}) async-start(), calls=%async_computation.1 | async-start | bytes 2752512 | tf_op jit(solution)/shard_map/psum | solution.py:27
  25.1 260.4 %all-reduce.4.cloned.1.call-start = ((), (), s32[]{:S(2)}) async-start(), calls=%async_computation | async-start | bytes 4194304 | tf_op jit(solution)/shard_map/psum | solution.py:41
  221.7 6.1 %copy-start.3 = (f32[256,256]{1,0:T(8,128)S(1)}, f32[256,256]{1,0:T(8,128)}, u32[]{:S(2)}) copy-start(f32[256,256]{1,0:T(8,128)} %param.16) | copy-start | bytes 786436
  285.5 8.7 %copy-start.2 = (f32[256,512]{1,0:T(8,128)S(1)}, f32[256,512]{1,0:T(8,128)}, u32[]{:S(2)}) copy-start(f32[256,512]{1,0:T(8,128)} %fusion.2) | copy-start | bytes 1572868
  285.5 10.6 %copy-start.1 = (f32[2048,256]{1,0:T(8,128)S(1)}, f32[2048,256]{1,0:T(8,128)}, u32[]{:S(2)}) copy-start(f32[2048,256]{1,0:T(8,128)} %all-reduce.4.cloned.1.call-done) | copy-start | bytes 6291460
  294.1 5.9 %copy-start.4 = (f32[256,64]{0,1:T(8,128)S(1)}, f32[256,64]{0,1:T(8,128)}, u32[]{:S(2)}) copy-start(f32[256,64]{0,1:T(8,128)} %get-tuple-element.55) | copy-start | bytes 196612
Sparse Core Ops, SparseCore 0:
  25.2 190.4 all-reduce.5
  221.8 63.6 all-reduce.3
where the time goes:
time: 308 us; the launch traced here: 307 us
  waiting for transfers between devices  244 us (79%)
  local copies, waits for them, and re-layouts  22.1 us (7%)
  matrix products  18.8 us (6%)
  between operations  14.2 us (5%)
  other arithmetic  8.61 us (3%)
    psum x1, waiting for transfers between devices, on_device(): lax.psum((sketch_part, panel_pick, look_pick, panel_head, look_head), 'row')  190 us
    psum x1, waiting for transfers between devices, on_device(): factor = lax.psum(partial_prod, 'col')  53.3 us
    unnamed x16, local copies, waits for them, and re-layouts  9.15 us
    dot_general x1, matrix products, on_device(): jnp.dot(factor, u_rows, precision=high_prec, preferred_element_type=jnp.f...  8.65 us
  transfers between devices with their start and end apart: 2, of which 2 were waited for; matrix products, arithmetic and copies ran while one was open for 3% of the time, Pallas kernels for 0%

commit v1 on v0

--- a/solution.py
+++ b/solution.py
@@ -38,7 +38,9 @@
     partial_prod = jnp.dot(
         swapped_panel, upper_rows, precision=high_prec, preferred_element_type=jnp.float32
     )
-    factor = lax.psum(partial_prod, "col")
+    factor = partial_prod
+    for hop in (1, 2):
+        factor = factor + lax.ppermute(factor, "col", [(dev, dev ^ hop) for dev in range(4)])
     global_row = first_row + jnp.arange(row_count, dtype=jnp.int32)
     is_top = (global_row < block_size)[:, None]
     my_factor = lax.dynamic_slice_in_dim(factor, col_index * col_width, col_width, 1)

time: 308 us -> 335 us (1.088)
  waiting for transfers between devices: 244 us -> 267 us
  matrix products: 18.8 us -> 11 us
  starting transfers between devices: 0.08 us -> 4.01 us
  other arithmetic: 8.61 us -> 12.4 us
    ppermute x0 -> x2, waiting for transfers between devices: none -> 77.7 us  [on_device(): lax.ppermute(factor, 'col', [(dev, dev ^ hop) for dev in range(4)])]
    psum x1 -> x0, waiting for transfers between devices: 53.3 us -> none  [on_device(): factor = lax.psum(partial_prod, 'col')]
    dot_general x1, matrix products: 8.65 us -> 3.67 us  [on_device(): jnp.dot(factor, u_rows, precision=high_prec, preferred_element_type=jnp.f...]
    add x0 -> x2, other arithmetic: none -> 4.05 us  [on_device(): factor + lax.ppermute(factor, 'col', [(dev, dev ^ hop) for dev in range(4)])]
    ppermute x0 -> x2, starting transfers between devices: none -> 3.97 us  [on_device(): lax.ppermute(factor, 'col', [(dev, dev ^ hop) for dev in range(4)])]
    unnamed x16 -> x21, local copies, waits for them, and re-layouts: 9.15 us -> 8.21 us
  transfers between devices with their start and end apart: 2 -> 3, of which waited for: 2 -> 3; matrix products, arithmetic and copies ran while one was open for 3% -> 3% of each run, Pallas kernels for 0% -> 0%
where the time goes in v1:
time: 335 us; the launch traced here: 331 us
  waiting for transfers between devices  267 us (80%)
  local copies, waits for them, and re-layouts  22.4 us (7%)
  between operations  14.2 us (4%)
  other arithmetic  12.4 us (4%)
  matrix products  11 us (3%)
  starting transfers between devices  4.01 us (1%)
    psum x1, waiting for transfers between devices, on_device(): lax.psum((sketch_part, panel_pick, look_pick, panel_head, look_head), 'row')  190 us
    ppermute x2, waiting for transfers between devices, on_device(): lax.ppermute(factor, 'col', [(dev, dev ^ hop) for dev in range(4)])  77.7 us
    unnamed x21, local copies, waits for them, and re-layouts  8.21 us
  transfers between devices with their start and end apart: 3, of which 3 were waited for; matrix products, arithmetic and copies ran while one was open for 3% of the time, Pallas kernels for 0%

profile of v1, /device:TPU:1, one launch (start us, length us, event | category | flops | bytes accessed | tf_op | source)
XLA Modules:
  0.0 331.4 jit_solution(15169233684660707983)
XLA Ops:
  7.2 0.0 copy-start
  7.2 0.0 all-reduce.3.cloned.1.call-start
  7.2 4.8 %copy.30 = f32[2048,512]{1,0:T(8,128)} copy(f32[2048,512]{1,0:T(8,128)} %param.13) | data formatting | bytes 8388608
  12.1 1.4 copy.11
  13.5 3.7 %fusion.14 = f32[256,64]{0,1:T(8,128)} fusion(f32[256,2048]{1,0:T(8,128)S(1)} %copy-done, f32[2048,64]{0,1:T(8,128)} %param.12), kind=kOutput, calls=%fused_computation.36 | convolution fusion | flops 402653184 | bytes 2686976 | tf_op jit(solution)/shard_map/dot_general | solution.py:21
  17.2 0.7 gather_fusion
  17.9 0.1 copy.14
  18.0 4.2 %gather_fusion.1 = f32[256,512]{1,0:T(8,128)} fusion(f32[2048,512]{1,0:T(8,128)} %copy.30, s32[1024]{0:T(1024)S(1)} %pad_clamp_fusion), kind=kCustom, calls=%fused_computation.1 | custom fusion | bytes 1049600 | tf_op jit(solution)/shard_map/gather | solution.py:20
  22.2 1.5 slice_select_fusion.4
  23.6 2.2 slice_select_fusion.2
  25.9 0.0 all-reduce.3.cloned.1.call-update
  25.9 0.1 iota_compare_fusion.1
  26.0 189.7 %all-reduce.3.cloned.1.call-done = (f32[256,64]{0,1:T(8,128)}, f32[256,64]{0,1:T(8,128)}, f32[256,512]{1,0:T(8,128)}, f32[256,512]{1,0:T(8,128)}, f32[256,64]{0,1:T(8,128)}) async-done(((f32[256,64]{0,1:T(8,128)}, f32[256,64]{0,1:T(8,128)}, f32[256,512]{1,0:T(8,128)}, f32[256,512]{1,0:T(8,128)}, f32[256,64]{0,1:T(8,128)}), (f32[256,64]{0,1:T(8,128)}, f32[256,64]{0,1:T(8,128)}, f32[256,512]{1,0:T(8,128)}, ...) | async-done | bytes 1245200 | tf_op jit(solution)/shard_map/psum | solution.py:27
  215.7 0.9 copy.12
  216.7 1.6 scatter_fusion
  218.2 1.1 copy.16
  219.3 1.5 fusion.8
  220.8 2.9 fusion.7
  223.8 1.3 collective-permute-start
  225.0 43.3 %collective-permute-done = f32[2048,256]{0,1:T(8,128)S(1)} collective-permute-done((f32[2048,256]{0,1:T(8,128)S(1)}, f32[2048,256]{0,1:T(8,128)S(1)}, u32[]{:S(2)}, u32[]{:S(2)}) %collective-permute-start) | collective-permute-done | bytes 2097184 | tf_op jit(solution)/shard_map/ppermute | solution.py:43
  268.4 1.6 add.73
  270.0 2.7 collective-permute-start.1
  272.7 5.6 %scatter_fusion.1 = f32[2048,512]{1,0:T(8,128)} fusion(f32[2048,512]{1,0:T(8,128)} %copy.30, s32[256]{0:T(256)S(1)} %get-tuple-element.45, f32[256,512]{1,0:T(8,128)S(1)} %copy-done.5), kind=kCustom, calls=%fused_computation.3 | custom fusion | bytes 1573888 | tf_op jit(solution)/shard_map/scatter | solution.py:32
  278.3 0.7 fusion.2
  279.0 2.0 fusion.1
  281.0 34.4 %collective-permute-done.1 = f32[2048,256]{0,1:T(8,128)} collective-permute-done((f32[2048,256]{0,1:T(8,128)}, f32[2048,256]{0,1:T(8,128)}, u32[]{:S(2)}, u32[]{:S(2)}) %collective-permute-start.1) | collective-permute-done | bytes 2097184 | tf_op jit(solution)/shard_map/ppermute | solution.py:43
  315.4 2.5 add.74
  317.9 0.9 dynamic-slice_select_fusion
  318.7 3.7 %convolution_subtract_fusion = f32[2048,512]{1,0:T(8,128)S(1)} fusion(f32[2048,512]{1,0:T(8,128)S(1)} %copy-done.1, f32[2048,256]{0,1:T(8,128)S(1)} %add.74, f32[256,512]{1,0:T(8,128)S(1)} %fusion.2), kind=kOutput, calls=%fused_computation.4 | convolution fusion | flops 3222274048 | bytes 11010048 | tf_op jit(solution)/shard_map/dot_general | solution.py:49
  322.4 0.1 fusion
  322.6 0.7 copy.31
  323.3 1.3 copy-done.2
  (21 shorter events, 0.1 us)
Async XLA Ops:
  7.2 6.3 %copy-start = (f32[256,2048]{1,0:T(8,128)S(1)}, f32[256,2048]{1,0:T(8,128)}, u32[]{:S(2)}) copy-start(f32[256,2048]{1,0:T(8,128)} %param.14) | copy-start | bytes 6291460
  7.2 4.8 %copy-start.8 = (s32[256]{0:T(256)S(1)}, s32[256]{0:T(256)}, u32[]{:S(2)}) copy-start(s32[256]{0:T(256)} %param.17) | copy-start | bytes 3076
  7.2 208.5 %all-reduce.3.cloned.1.call-start = ((), (), s32[]{:S(2)}) async-start(), calls=%async_computation | async-start | bytes 2490368 | tf_op jit(solution)/shard_map/psum | solution.py:27
  220.8 51.9 %copy-start.5 = (f32[256,512]{1,0:T(8,128)S(1)}, f32[256,512]{1,0:T(8,128)}, u32[]{:S(2)}) copy-start(f32[256,512]{1,0:T(8,128)} %get-tuple-element.41) | copy-start | bytes 1572868
  223.8 44.6 %collective-permute-start = (f32[2048,256]{0,1:T(8,128)S(1)}, f32[2048,256]{0,1:T(8,128)S(1)}, u32[]{:S(2)}, u32[]{:S(2)}) collective-permute-start(f32[2048,256]{0,1:T(8,128)S(1)} %fusion.7), channel_id=1, source_target_pairs={{0,1},{1,0},{2,3},{3,2},{4,5},{5,4},{6,7},{7,6},{8,9},{9,8},{10,11... | collective-permute-start | bytes 6291464 | tf_op jit(solution)/shard_map/ppermute | solution.py:43
  270.0 45.4 %collective-permute-start.1 = (f32[2048,256]{0,1:T(8,128)}, f32[2048,256]{0,1:T(8,128)}, u32[]{:S(2)}, u32[]{:S(2)}) collective-permute-start(f32[2048,256]{0,1:T(8,128)} %add.73), channel_id=1, source_target_pairs={{0,2},{1,3},{2,0},{3,1},{4,6},{5,7},{6,4},{7,5},{8,10},{9,11},{10,... | collective-permute-start | bytes 6291464 | tf_op jit(solution)/shard_map/ppermute | solution.py:43
  272.7 5.7 %copy-start.4 = (f32[256,512]{1,0:T(8,128)S(1)}, f32[256,512]{1,0:T(8,128)}, u32[]{:S(2)}) copy-start(f32[256,512]{1,0:T(8,128)} %get-tuple-element.42) | copy-start | bytes 1572868
  272.7 5.7 %copy-start.6 = (f32[256,256]{1,0:T(8,128)S(1)}, f32[256,256]{1,0:T(8,128)}, u32[]{:S(2)}) copy-start(f32[256,256]{1,0:T(8,128)} %param.16) | copy-start | bytes 786436
  279.0 38.9 %copy-start.3 = (f32[2048,64]{0,1:T(8,128)S(1)}, f32[2048,64]{0,1:T(8,128)}, u32[]{:S(2)}) copy-start(f32[2048,64]{0,1:T(8,128)} %fusion.8) | copy-start | bytes 1572868
  281.0 37.7 %copy-start.1 = (f32[2048,512]{1,0:T(8,128)S(1)}, f32[2048,512]{1,0:T(8,128)}, u32[]{:S(2)}) copy-start(f32[2048,512]{1,0:T(8,128)} %fusion.1) | copy-start | bytes 12582916
  318.7 3.8 %copy-start.7 = (f32[256,64]{0,1:T(8,128)S(1)}, f32[256,64]{0,1:T(8,128)}, u32[]{:S(2)}) copy-start(f32[256,64]{0,1:T(8,128)} %get-tuple-element.52) | copy-start | bytes 196612
  322.6 2.0 copy-start.2
Sparse Core Ops, SparseCore 0:
  26.0 189.6 all-reduce.2
